TPU v7x, 32 devices: a whole 2x2x4 slice. The times are simulated.
32 devices in a mesh: grp: 2 (over y), bits: 4 (over z), tgt: 2 (over x), sub: 2 (over core).
Axes of the slice: x: 2, y: 2, z: 4, core: 2. Of those that a mesh axis runs over, the one named last changes fastest.
Arguments:
- coefficients: bfloat16 [16, 8192, 128], P(('grp', 'bits', 'sub'), 'tgt'), parts along dimension 0, may hold values from -6 to 6
- patterns: int32 [2, 16, 8192], P(None, ('grp', 'bits', 'sub'), 'tgt'), parts along dimension 1, may hold values from 0 to 65535
- blocks: bfloat16 [2, 16, 2048, 128], P(None, ('grp', 'bits', 'sub')), parts along dimension 1, may hold values from -0.1875 to 0.1875
- box_index: int32 [16], P(('grp', 'bits', 'sub')), parts along dimension 0, may hold values from 0 to 4095
- target_index: int32 [16384], P(('grp', 'tgt')), parts along dimension 0, may hold values from 0 to 4095
- partner_bits: int32 [4], P('grp'), parts along dimension 0, may hold values from 0 to 2, as said below
- evaluation: bfloat16 [128, 8192], replicated, may hold values from -0.0625 to 0.0625
Outputs:
- values: float32 [16, 128, 128], P(('grp', 'bits', 'sub'), 'tgt'), parts along dimension 0
There are 2 independent parts, one for each index of `grp`. A program takes and returns all parts, laid end to end along the dimension named above; an argument that names none is the same for every part. Nothing has to cross between parts.
Inputs may be any that keep to these rules, and one draw needn't show every extreme that they name: `partner_bits`: two different bits of a box number; the highest bit 3 - 1 is always one of them.
All inputs are finite; a program needn't handle non-finite values.
Results may differ from a plain program's by a relative error of at most 0.0042.
Values may be sent and summed in bfloat16 or wider, within the bound.
A program may use at most 64 MiB of HBM per device.

v0:
```python
from functools import partial
import math

import jax
import jax.numpy as jnp
from jax import lax
from jax.experimental import pallas as pl
from jax.experimental.pallas import tpu as pltpu
from jax.sharding import PartitionSpec as P

GROUP = 128
CHUNK = 256
LAG = 4
MESH = pl.DeviceIdType.MESH


def column_of(row, rows, width):
    return jnp.transpose(jnp.broadcast_to(row, (width, rows)))


def cos_sin(turns):
    quarter = (turns + 512) >> 10
    x = (turns - (quarter << 10)).astype(jnp.float32) * (2.0 * math.pi / 4096.0)
    y = x * x
    s = x * (1.0 + y * (-1.0 / 6 + y * (1.0 / 120 + y * (-1.0 / 5040 + y * (1.0 / 362880)))))
    c = 1.0 + y * (-0.5 + y * (1.0 / 24 + y * (-1.0 / 720 + y * (1.0 / 40320 - y * (1.0 / 3628800)))))
    odd = (quarter & 1) == 1
    cos = jnp.where(odd, s, c)
    sin = jnp.where(odd, c, s)
    turn = quarter & 3
    cos = jnp.where((turn == 1) | (turn == 2), -cos, cos)
    sin = jnp.where((turn == 2) | (turn == 3), -sin, sin)
    return cos, sin


def mix(own, partner, pattern, weight, cos, sin):
    rows, width = own.shape
    terms = weight.shape[0] // width
    half = width // 2
    own32 = own.astype(jnp.float32)
    partner32 = partner.astype(jnp.float32)
    parts = []
    for k in range(terms):
        source = own32 if k < terms // 2 else partner32
        parts.append(jnp.where((pattern & (1 << k)) != 0, source, 0.0).astype(jnp.bfloat16))
    mixed = jnp.dot(jnp.concatenate(parts, axis=1), weight, preferred_element_type=jnp.float32)
    lane = lax.broadcasted_iota(jnp.int32, (rows, width), 1)
    signed = jnp.where(lane < half, -sin, sin)
    return (mixed * cos + pltpu.roll(mixed, half, 1) * signed).astype(jnp.bfloat16)


def kernel(top_first, sizes, box, bits, patterns, targets, weights, state0, evaluation, out,
           state1, arrived, trig, points_eval, total, sums,
           send_sem, recv_sem, eval_sem, sum_send, sum_recv):
    grp_n, bits_n, tgt_n, sub_n = sizes
    rows, width = state0.shape
    chunks = rows // CHUNK
    groups = CHUNK // GROUP
    levels = weights.shape[0]
    boxes = bits_n * sub_n
    lower = boxes.bit_length() - 2
    grp, tgt = lax.axis_index("grp"), lax.axis_index("tgt")
    me = lax.axis_index("bits") * sub_n + lax.axis_index("sub")
    if all(top_first):
        first = 1
    elif not any(top_first):
        first = 0
    else:
        first = sum(jnp.where(grp == g, 1, 0) for g in range(grp_n) if top_first[g])

    def across(stride):
        other = me + stride - 2 * stride * ((me // stride) % 2)
        return (grp, other // sub_n, tgt, other % sub_n)

    def at_tgt(t):
        return (grp, lax.axis_index("bits"), t, lax.axis_index("sub"))

    peers = [across(1 << j) for j in range(lower + 1)]
    peers += [at_tgt((tgt + d) % tgt_n) for d in range(1, tgt_n)]
    barrier = pltpu.get_barrier_semaphore()
    for peer in peers:
        pl.semaphore_signal(barrier, inc=1, device_id=peer, device_id_type=MESH)

    load_eval = pltpu.make_async_copy(
        evaluation.at[:, pl.ds(pl.multiple_of(tgt * rows, rows), rows)], points_eval, eval_sem)
    load_eval.start()

    pl.semaphore_wait(barrier, len(peers))

    def is_top(level):
        return first if level == 0 else 1 - first

    def copy(level, slot, c):
        source = state0 if level == 0 else state1
        span = pl.ds(pl.multiple_of(c * CHUNK, CHUNK), CHUNK)
        stride = 1 << slot
        if slot == 0:
            stride = 1 + is_top(level) * ((1 << lower) - 1)
        return pltpu.make_async_remote_copy(
            src_ref=source.at[span],
            dst_ref=arrived.at[level, slot, span],
            send_sem=send_sem.at[level, slot, c],
            recv_sem=recv_sem.at[level, slot, c],
            device_id=across(stride),
            device_id_type=MESH,
        )

    def each_copy(level, c, act):
        act(copy(level, 0, c))
        top = is_top(level)
        if isinstance(top, int):
            if not top:
                for slot in range(1, lower):
                    act(copy(level, slot, c))
        elif lower > 1:
            @pl.when(top == 0)
            def _():
                for slot in range(1, lower):
                    act(copy(level, slot, c))

    @pl.loop(0, chunks)
    def _(c):
        each_copy(0, c, lambda k: k.start())

    for level in range(levels):
        turns = (targets[...] * (box[0] * (level + 1))) & 4095
        cos, sin = cos_sin(turns)
        trig[level, 0] = cos
        trig[level, 1] = sin
    total[...] = jnp.zeros_like(total)
    load_eval.wait()

    def advance(level, c):
        each_copy(level, c, lambda k: k.wait_recv())
        span = pl.ds(pl.multiple_of(c * CHUNK, CHUNK), CHUNK)
        own = (state0 if level == 0 else state1)[span, :]
        partner = arrived[level, 0, span, :]
        for slot in range(1, lower):
            partner = jnp.where(bits[level] == slot, arrived[level, slot, span, :], partner)

        def column(ref, *lead):
            return jnp.concatenate(
                [column_of(ref[(*lead, pl.ds(c * groups + g, 1), slice(None))], GROUP, width)
                 for g in range(groups)], axis=0)

        return mix(own, partner, column(patterns, level), weights[level],
                   column(trig, level, 0), column(trig, level, 1))

    @pl.loop(0, chunks + LAG)
    def _(i):
        @pl.when(i < chunks)
        def _():
            state1[pl.ds(pl.multiple_of(i * CHUNK, CHUNK), CHUNK), :] = advance(0, i)
            each_copy(1, i, lambda k: k.start())

        @pl.when(i >= LAG)
        def _():
            c = i - LAG
            span = pl.ds(pl.multiple_of(c * CHUNK, CHUNK), CHUNK)
            total[...] += jnp.dot(points_eval[:, span], advance(1, c), preferred_element_type=jnp.float32)

    piece = out.shape[0]

    def sum_copy(d):
        peer = (tgt + d) % tgt_n
        return pltpu.make_async_remote_copy(
            src_ref=total.at[pl.ds(pl.multiple_of(peer * piece, piece), piece)],
            dst_ref=sums.at[d - 1],
            send_sem=sum_send.at[d - 1],
            recv_sem=sum_recv.at[d - 1],
            device_id=at_tgt(peer),
            device_id_type=MESH,
        )

    for d in range(1, tgt_n):
        sum_copy(d).start()

    @pl.loop(0, chunks)
    def _(c):
        for level in range(levels):
            each_copy(level, c, lambda k: k.wait_send())

    result = total[pl.ds(pl.multiple_of(tgt * piece, piece), piece), :]
    for d in range(1, tgt_n):
        sum_copy(d).wait()
        result = result + sums[d - 1]
    out[...] = result


def run(top_first, number, sizes, box, bits, patterns, targets, weights, state, evaluation):
    rows, width = state.shape
    levels = weights.shape[0]
    points = evaluation.shape[0]
    lower = (sizes[1] * sizes[3]).bit_length() - 2
    slots = max(lower, 1)
    chunks = rows // CHUNK
    others = max(sizes[2] - 1, 1)
    smem = pl.BlockSpec(memory_space=pltpu.SMEM)
    vmem = pl.BlockSpec(memory_space=pltpu.VMEM)
    return pl.pallas_call(
        partial(kernel, top_first, sizes),
        out_shape=jax.ShapeDtypeStruct((points // sizes[2], width), jnp.float32),
        in_specs=[smem, smem, vmem, vmem, vmem, vmem, pl.BlockSpec(memory_space=pl.ANY)],
        out_specs=vmem,
        scratch_shapes=[
            pltpu.VMEM((rows, width), jnp.bfloat16),
            pltpu.VMEM((levels, slots, rows, width), jnp.bfloat16),
            pltpu.VMEM((levels, 2, rows // GROUP, GROUP), jnp.float32),
            pltpu.VMEM((points, rows), jnp.bfloat16),
            pltpu.VMEM((points, width), jnp.float32),
            pltpu.VMEM((others, points // sizes[2], width), jnp.float32),
            pltpu.SemaphoreType.DMA((levels, slots, chunks)),
            pltpu.SemaphoreType.DMA((levels, slots, chunks)),
            pltpu.SemaphoreType.DMA,
            pltpu.SemaphoreType.DMA((others,)),
            pltpu.SemaphoreType.DMA((others,)),
        ],
        cost_estimate=pl.CostEstimate(
            flops=2 * levels * rows * weights.shape[1] * width, bytes_accessed=8 << 20, transcendentals=0),
        compiler_params=pltpu.CompilerParams(
            collective_id=number, has_side_effects=True, vmem_limit_bytes=40 << 20),
    )(box, bits, patterns, targets, weights, state, evaluation)


def body(sizes, coefficients, patterns, blocks, box_index, target_index, partner_bits, evaluation):
    state = coefficients[0]
    rows = state.shape[0]
    levels = patterns.shape[0]
    pattern_rows = patterns.reshape(levels, rows // GROUP, GROUP)
    targets = target_index.reshape(rows // GROUP, GROUP)

    grp_n = sizes[0]
    mine = lax.axis_index("grp")
    top = (sizes[1] * sizes[3]).bit_length() - 2

    def flag(bits):
        return (bits[0] == top).astype(jnp.int32)

    which = flag(partner_bits) << mine
    for apart in range(1, grp_n):
        theirs = lax.ppermute(partner_bits, "grp", [(g, (g + apart) % grp_n) for g in range(grp_n)])
        which = which + (flag(theirs) << ((mine - apart) % grp_n))
    variants = [tuple(bool(v >> g & 1) for g in range(grp_n)) for v in range(1 << grp_n)]
    result = lax.switch(
        which, [partial(run, variant, v, sizes) for v, variant in enumerate(variants)],
        box_index, partner_bits, pattern_rows, targets, blocks[:, 0], state, evaluation)
    return result[None]


def solution(mesh):
    sizes = tuple(mesh.shape[name] for name in ("grp", "bits", "tgt", "sub"))
    in_specs = (
        P(("grp", "bits", "sub"), "tgt", None),
        P(None, ("grp", "bits", "sub"), "tgt"),
        P(None, ("grp", "bits", "sub"), None, None),
        P(("grp", "bits", "sub")),
        P(("grp", "tgt")),
        P("grp"),
        P(),
    )
    out_specs = P(("grp", "bits", "sub"), "tgt", None)
    return jax.shard_map(
        partial(body, sizes), mesh=mesh, in_specs=in_specs, out_specs=out_specs, check_vma=False)
```

profile of v0, /device:TPU:0, one launch (start us, length us, event | category | flops | bytes accessed | tf_op | source)
XLA Modules:
  0.0 77.8 jit_solution(5591212384850066817)
XLA Ops:
  0.0 3.0 %collective-permute-start = (s32[2]{0:T(128)}, s32[2]{0:T(128)S(1)}, u32[]{:S(2)}, u32[]{:S(2)}) collective-permute-start(s32[2]{0:T(128)} %param.16), channel_id=1, source_target_pairs={{0,16},{16,0},{1,17},{17,1},{2,18},{18,2},{3,19},{19,3},{4,20},{20... | collective-permute-start | bytes 32 | tf_op jit(solution)/shard_map/ppermute | solution.py:241
  3.7 1.0 %collective-permute-done = s32[2]{0:T(128)S(1)} collective-permute-done((s32[2]{0:T(128)}, s32[2]{0:T(128)S(1)}, u32[]{:S(2)}, u32[]{:S(2)}) %collective-permute-start) | collective-permute-done | bytes 40 | tf_op jit(solution)/shard_map/ppermute | solution.py:241
  4.7 72.5 %conditional.1 = (f32[1,64,128]{2,1,0:T(8,128)S(1)}) conditional(s32[]{:T(128)} %clamp.3, (s32[1]{0:T(128)}, s32[2]{0:T(128)}, s32[2,32,128]{2,1,0:T(8,128)}, s32[32,128]{1,0:T(8,128)}, bf16[2,2048,128]{2,1,0:T(8,128)(2,1)}, /*index=5*/bf16[4096,128]{1,0:T(8,128)(2,1)}, bf16[128,8192]{1,0:T(8,128)(2,1)}) %tuple.42, ...), branch_computations={%region_0.1_spmd, %region_1.2_spmd, %region_2.3_spmd, %region_3.4_... | conditional | flops 4294967296 | bytes 8388616 | solution.py:244
  4.7 72.5 %branch_1_fun.1 = f32[64,128]{1,0:T(8,128)S(1)} custom-call(s32[1]{0:T(128)} %get-tuple-element.74.box, s32[2]{0:T(128)} %get-tuple-element.75.bits, s32[2,32,128]{2,1,0:T(8,128)} %get-tuple-element.76.patterns, s32[32,128]{1,0:T(8,128)} %get-tuple-element.77.targets, bf16[2,2048,128]{2,1,0:T(8,128)(2,1)} %get-tuple-element.78.weights, ...), custom_call_target="tpu_custom_call" | custom-call | flops 4294967296 | bytes 8388608 | tf_op jit(solution)/shard_map/cond/branch_1_fun/pallas_call | solution.py:200
  77.2 0.6 copy.17
Async XLA Ops:
  0.0 4.6 %collective-permute-start = (s32[2]{0:T(128)}, s32[2]{0:T(128)S(1)}, u32[]{:S(2)}, u32[]{:S(2)}) collective-permute-start(s32[2]{0:T(128)} %param.16), channel_id=1, source_target_pairs={{0,16},{16,0},{1,17},{17,1},{2,18},{18,2},{3,19},{19,3},{4,20},{20... | collective-permute-start | bytes 32 | tf_op jit(solution)/shard_map/ppermute | solution.py:241
where the time goes:
time: 78 us; the launch traced here: 77.8 us
  Pallas kernels  72.5 us (93%)
  starting transfers between devices  2.97 us (4%)
  waiting for transfers between devices  0.96 us (1%)
    pallas_call x1, Pallas kernels, run(): pl.pallas_call(partial(kernel, top_first, sizes), out_shape=jax.ShapeDtyp...  72.5 us
    ppermute x1, starting transfers between devices, body(): lax.ppermute(partner_bits, 'grp', [(g, (g + apart) % grp_n) for g in rang...  2.97 us
  transfers between devices with their start and end apart: 1, of which 1 were waited for; matrix products, arithmetic and copies ran while one was open for 0% of the time, Pallas kernels for 0%

commit v1 on v0

--- a/solution.py
+++ b/solution.py
@@ -10,7 +10,8 @@
 
 GROUP = 128
 CHUNK = 256
-LAG = 4
+LAG = 2
+WINDOW = 3
 MESH = pl.DeviceIdType.MESH
 
 
@@ -118,7 +119,7 @@
                 for slot in range(1, lower):
                     act(copy(level, slot, c))
 
-    @pl.loop(0, chunks)
+    @pl.loop(0, min(WINDOW, chunks))
     def _(c):
         each_copy(0, c, lambda k: k.start())
 
@@ -132,6 +133,10 @@
 
     def advance(level, c):
         each_copy(level, c, lambda k: k.wait_recv())
+        if level == 0:
+            @pl.when(c + WINDOW < chunks)
+            def _():
+                each_copy(0, c + WINDOW, lambda k: k.start())
         span = pl.ds(pl.multiple_of(c * CHUNK, CHUNK), CHUNK)
         own = (state0 if level == 0 else state1)[span, :]
         partner = arrived[level, 0, span, :]

time: 78 us -> 67 us (0.86)
  Pallas kernels: 72.5 us -> 61.5 us
    pallas_call x1, Pallas kernels: 72.5 us -> 61.5 us  [run(): pl.pallas_call(partial(kernel, top_first, sizes), out_shape=jax.ShapeDtyp...]
where the time goes in v1:
time: 67 us; the launch traced here: 66.9 us
  Pallas kernels  61.5 us (92%)
  starting transfers between devices  2.97 us (4%)
  waiting for transfers between devices  0.96 us (1%)
  between operations  0.75 us (1%)
    pallas_call x1, Pallas kernels, run(): pl.pallas_call(partial(kernel, top_first, sizes), out_shape=jax.ShapeDtyp...  61.5 us
    ppermute x1, starting transfers between devices, body(): lax.ppermute(partner_bits, 'grp', [(g, (g + apart) % grp_n) for g in rang...  2.97 us
  transfers between devices with their start and end apart: 1, of which 1 were waited for; matrix products, arithmetic and copies ran while one was open for 0% of the time, Pallas kernels for 0%

profile of v1, /device:TPU:0, one launch (start us, length us, event | category | flops | bytes accessed | tf_op | source)
XLA Modules:
  0.0 66.9 jit_solution(17082048368079929700)
XLA Ops:
  0.0 3.0 %collective-permute-start = (s32[2]{0:T(128)}, s32[2]{0:T(128)S(1)}, u32[]{:S(2)}, u32[]{:S(2)}) collective-permute-start(s32[2]{0:T(128)} %param.16), channel_id=1, source_target_pairs={{0,16},{16,0},{1,17},{17,1},{2,18},{18,2},{3,19},{19,3},{4,20},{20... | collective-permute-start | bytes 32 | tf_op jit(solution)/shard_map/ppermute | solution.py:246
  3.7 1.0 %collective-permute-done = s32[2]{0:T(128)S(1)} collective-permute-done((s32[2]{0:T(128)}, s32[2]{0:T(128)S(1)}, u32[]{:S(2)}, u32[]{:S(2)}) %collective-permute-start) | collective-permute-done | bytes 40 | tf_op jit(solution)/shard_map/ppermute | solution.py:246
  4.7 61.6 %conditional.1 = (f32[1,64,128]{2,1,0:T(8,128)S(1)}) conditional(s32[]{:T(128)} %clamp.3, (s32[1]{0:T(128)}, s32[2]{0:T(128)}, s32[2,32,128]{2,1,0:T(8,128)}, s32[32,128]{1,0:T(8,128)}, bf16[2,2048,128]{2,1,0:T(8,128)(2,1)}, /*index=5*/bf16[4096,128]{1,0:T(8,128)(2,1)}, bf16[128,8192]{1,0:T(8,128)(2,1)}) %tuple.42, ...), branch_computations={%region_0.1_spmd, %region_1.2_spmd, %region_2.3_spmd, %region_3.4_... | conditional | flops 4294967296 | bytes 8388616 | solution.py:249
  4.7 61.5 %branch_0_fun.1 = f32[64,128]{1,0:T(8,128)S(1)} custom-call(s32[1]{0:T(128)} %get-tuple-element.66.box, s32[2]{0:T(128)} %get-tuple-element.68.bits, s32[2,32,128]{2,1,0:T(8,128)} %get-tuple-element.69.patterns, s32[32,128]{1,0:T(8,128)} %get-tuple-element.70.targets, bf16[2,2048,128]{2,1,0:T(8,128)(2,1)} %get-tuple-element.71.weights, ...), custom_call_target="tpu_custom_call" | custom-call | flops 4294967296 | bytes 8388608 | tf_op jit(solution)/shard_map/cond/branch_0_fun/pallas_call | solution.py:205
  66.2 0.6 copy.17
Async XLA Ops:
  0.0 4.6 %collective-permute-start = (s32[2]{0:T(128)}, s32[2]{0:T(128)S(1)}, u32[]{:S(2)}, u32[]{:S(2)}) collective-permute-start(s32[2]{0:T(128)} %param.16), channel_id=1, source_target_pairs={{0,16},{16,0},{1,17},{17,1},{2,18},{18,2},{3,19},{19,3},{4,20},{20... | collective-permute-start | bytes 32 | tf_op jit(solution)/shard_map/ppermute | solution.py:246

commit v2 on v1

--- a/solution.py
+++ b/solution.py
@@ -50,9 +50,9 @@
     return (mixed * cos + pltpu.roll(mixed, half, 1) * signed).astype(jnp.bfloat16)
 
 
-def kernel(top_first, sizes, box, bits, patterns, targets, weights, state0, evaluation, out,
-           state1, arrived, trig, points_eval, total, sums,
-           send_sem, recv_sem, eval_sem, sum_send, sum_recv):
+def kernel(top_first, sizes, box, bits, patterns, targets, weights_hbm, state_hbm, evaluation, out,
+           state0, weights, state1, arrived, trig, points_eval, total, sums,
+           send_sem, recv_sem, eval_sem, load_sem, sum_send, sum_recv):
     grp_n, bits_n, tgt_n, sub_n = sizes
     rows, width = state0.shape
     chunks = rows // CHUNK
@@ -84,6 +84,10 @@
 
     load_eval = pltpu.make_async_copy(
         evaluation.at[:, pl.ds(pl.multiple_of(tgt * rows, rows), rows)], points_eval, eval_sem)
+    load_state = pltpu.make_async_copy(state_hbm, state0, load_sem.at[0])
+    load_weights = pltpu.make_async_copy(weights_hbm, weights, load_sem.at[1])
+    load_state.start()
+    load_weights.start()
     load_eval.start()
 
     pl.semaphore_wait(barrier, len(peers))
@@ -92,7 +96,7 @@
         return first if level == 0 else 1 - first
 
     def copy(level, slot, c):
-        source = state0 if level == 0 else state1
+        source = state_hbm if level == 0 else state1
         span = pl.ds(pl.multiple_of(c * CHUNK, CHUNK), CHUNK)
         stride = 1 << slot
         if slot == 0:
@@ -129,6 +133,8 @@
         trig[level, 0] = cos
         trig[level, 1] = sin
     total[...] = jnp.zeros_like(total)
+    load_state.wait()
+    load_weights.wait()
     load_eval.wait()
 
     def advance(level, c):
@@ -205,9 +211,11 @@
     return pl.pallas_call(
         partial(kernel, top_first, sizes),
         out_shape=jax.ShapeDtypeStruct((points // sizes[2], width), jnp.float32),
-        in_specs=[smem, smem, vmem, vmem, vmem, vmem, pl.BlockSpec(memory_space=pl.ANY)],
+        in_specs=[smem, smem, vmem, vmem] + [pl.BlockSpec(memory_space=pl.ANY)] * 3,
         out_specs=vmem,
         scratch_shapes=[
+            pltpu.VMEM((rows, width), jnp.bfloat16),
+            pltpu.VMEM(weights.shape, jnp.bfloat16),
             pltpu.VMEM((rows, width), jnp.bfloat16),
             pltpu.VMEM((levels, slots, rows, width), jnp.bfloat16),
             pltpu.VMEM((levels, 2, rows // GROUP, GROUP), jnp.float32),
@@ -217,6 +225,7 @@
             pltpu.SemaphoreType.DMA((levels, slots, chunks)),
             pltpu.SemaphoreType.DMA((levels, slots, chunks)),
             pltpu.SemaphoreType.DMA,
+            pltpu.SemaphoreType.DMA((2,)),
             pltpu.SemaphoreType.DMA((others,)),
             pltpu.SemaphoreType.DMA((others,)),
         ],

time: 67 us -> 66.3 us (0.990)
  Pallas kernels: 61.5 us -> 60.3 us
    pallas_call x1, Pallas kernels: 61.5 us -> 60.3 us  [run(): pl.pallas_call(partial(kernel, top_first, sizes), out_shape=jax.ShapeDtyp...]
where the time goes in v2:
time: 66.3 us; the launch traced here: 65.7 us
  Pallas kernels  60.3 us (91%)
  starting transfers between devices  2.97 us (4%)
  waiting for transfers between devices  0.96 us (1%)
  between operations  0.75 us (1%)
    pallas_call x1, Pallas kernels, run(): pl.pallas_call(partial(kernel, top_first, sizes), out_shape=jax.ShapeDtyp...  60.3 us
    ppermute x1, starting transfers between devices, body(): lax.ppermute(partner_bits, 'grp', [(g, (g + apart) % grp_n) for g in rang...  2.97 us
  transfers between devices with their start and end apart: 1, of which 1 were waited for; matrix products, arithmetic and copies ran while one was open for 0% of the time, Pallas kernels for 0%

profile of v2, /device:TPU:0, one launch (start us, length us, event | category | flops | bytes accessed | tf_op | source)
XLA Modules:
  0.0 65.7 jit_solution(9299604357853796035)
XLA Ops:
  0.0 3.0 %collective-permute-start = (s32[2]{0:T(128)}, s32[2]{0:T(128)S(1)}, u32[]{:S(2)}, u32[]{:S(2)}) collective-permute-start(s32[2]{0:T(128)} %param.16), channel_id=1, source_target_pairs={{0,16},{16,0},{1,17},{17,1},{2,18},{18,2},{3,19},{19,3},{4,20},{20... | collective-permute-start | bytes 32 | tf_op jit(solution)/shard_map/ppermute | solution.py:255
  3.7 1.0 %collective-permute-done = s32[2]{0:T(128)S(1)} collective-permute-done((s32[2]{0:T(128)}, s32[2]{0:T(128)S(1)}, u32[]{:S(2)}, u32[]{:S(2)}) %collective-permute-start) | collective-permute-done | bytes 40 | tf_op jit(solution)/shard_map/ppermute | solution.py:255
  4.7 60.4 %conditional.1 = (f32[1,64,128]{2,1,0:T(8,128)S(1)}) conditional(s32[]{:T(128)} %clamp.3, (s32[1]{0:T(128)}, s32[2]{0:T(128)}, s32[2,32,128]{2,1,0:T(8,128)}, s32[32,128]{1,0:T(8,128)}, bf16[2,2048,128]{2,1,0:T(8,128)(2,1)}, /*index=5*/bf16[4096,128]{1,0:T(8,128)(2,1)}, bf16[128,8192]{1,0:T(8,128)(2,1)}) %tuple.42, ...), branch_computations={%region_0.1_spmd, %region_1.2_spmd, %region_2.3_spmd, %region_3.4_... | conditional | flops 4294967296 | bytes 8388616 | solution.py:258
  4.7 60.3 %branch_0_fun.1 = f32[64,128]{1,0:T(8,128)S(1)} custom-call(s32[1]{0:T(128)} %get-tuple-element.66.box, s32[2]{0:T(128)} %get-tuple-element.68.bits, s32[2,32,128]{2,1,0:T(8,128)} %get-tuple-element.69.patterns, s32[32,128]{1,0:T(8,128)} %get-tuple-element.70.targets, bf16[2,2048,128]{2,1,0:T(8,128)(2,1)} %get-tuple-element.71.weights_hbm, ...), custom_call_target="tpu_custom_call" | custom-call | flops 4294967296 | bytes 8388608 | tf_op jit(solution)/shard_map/cond/branch_0_fun/pallas_call | solution.py:211
  65.0 0.6 copy.17
Async XLA Ops:
  0.0 4.6 %collective-permute-start = (s32[2]{0:T(128)}, s32[2]{0:T(128)S(1)}, u32[]{:S(2)}, u32[]{:S(2)}) collective-permute-start(s32[2]{0:T(128)} %param.16), channel_id=1, source_target_pairs={{0,16},{16,0},{1,17},{17,1},{2,18},{18,2},{3,19},{19,3},{4,20},{20... | collective-permute-start | bytes 32 | tf_op jit(solution)/shard_map/ppermute | solution.py:255

commit v3 on v2

--- a/solution.py
+++ b/solution.py
@@ -163,12 +163,14 @@
         def _():
             state1[pl.ds(pl.multiple_of(i * CHUNK, CHUNK), CHUNK), :] = advance(0, i)
             each_copy(1, i, lambda k: k.start())
+            each_copy(0, i, lambda k: k.wait_send())
 
         @pl.when(i >= LAG)
         def _():
             c = i - LAG
             span = pl.ds(pl.multiple_of(c * CHUNK, CHUNK), CHUNK)
             total[...] += jnp.dot(points_eval[:, span], advance(1, c), preferred_element_type=jnp.float32)
+            each_copy(1, c, lambda k: k.wait_send())
 
     piece = out.shape[0]
 
@@ -185,11 +187,6 @@
 
     for d in range(1, tgt_n):
         sum_copy(d).start()
-
-    @pl.loop(0, chunks)
-    def _(c):
-        for level in range(levels):
-            each_copy(level, c, lambda k: k.wait_send())
 
     result = total[pl.ds(pl.multiple_of(tgt * piece, piece), piece), :]
     for d in range(1, tgt_n):

time: 66.3 us -> 66.7 us (level)
  Pallas kernels: 60.3 us -> 61.1 us
    pallas_call x1, Pallas kernels: 60.3 us -> 61.1 us  [run(): pl.pallas_call(partial(kernel, top_first, sizes), out_shape=jax.ShapeDtyp...]
where the time goes in v3:
time: 66.7 us; the launch traced here: 66.4 us
  Pallas kernels  61.1 us (92%)
  starting transfers between devices  2.97 us (4%)
  waiting for transfers between devices  0.96 us (1%)
  between operations  0.75 us (1%)
    pallas_call x1, Pallas kernels, run(): pl.pallas_call(partial(kernel, top_first, sizes), out_shape=jax.ShapeDtyp...  61.1 us
    ppermute x1, starting transfers between devices, body(): lax.ppermute(partner_bits, 'grp', [(g, (g + apart) % grp_n) for g in rang...  2.97 us
  transfers between devices with their start and end apart: 1, of which 1 were waited for; matrix products, arithmetic and copies ran while one was open for 0% of the time, Pallas kernels for 0%

profile of v3, /device:TPU:0, one launch (start us, length us, event | category | flops | bytes accessed | tf_op | source)
XLA Modules:
  0.0 66.4 jit_solution(11975471453095104035)
XLA Ops:
  0.0 3.0 %collective-permute-start = (s32[2]{0:T(128)}, s32[2]{0:T(128)S(1)}, u32[]{:S(2)}, u32[]{:S(2)}) collective-permute-start(s32[2]{0:T(128)} %param.16), channel_id=1, source_target_pairs={{0,16},{16,0},{1,17},{17,1},{2,18},{18,2},{3,19},{19,3},{4,20},{20... | collective-permute-start | bytes 32 | tf_op jit(solution)/shard_map/ppermute | solution.py:252
  3.7 1.0 %collective-permute-done = s32[2]{0:T(128)S(1)} collective-permute-done((s32[2]{0:T(128)}, s32[2]{0:T(128)S(1)}, u32[]{:S(2)}, u32[]{:S(2)}) %collective-permute-start) | collective-permute-done | bytes 40 | tf_op jit(solution)/shard_map/ppermute | solution.py:252
  4.7 61.1 %conditional.1 = (f32[1,64,128]{2,1,0:T(8,128)S(1)}) conditional(s32[]{:T(128)} %clamp.3, (s32[1]{0:T(128)}, s32[2]{0:T(128)}, s32[2,32,128]{2,1,0:T(8,128)}, s32[32,128]{1,0:T(8,128)}, bf16[2,2048,128]{2,1,0:T(8,128)(2,1)}, /*index=5*/bf16[4096,128]{1,0:T(8,128)(2,1)}, bf16[128,8192]{1,0:T(8,128)(2,1)}) %tuple.42, ...), branch_computations={%region_0.1_spmd, %region_1.2_spmd, %region_2.3_spmd, %region_3.4_... | conditional | flops 4294967296 | bytes 8388616 | solution.py:255
  4.7 61.1 %branch_1_fun.1 = f32[64,128]{1,0:T(8,128)S(1)} custom-call(s32[1]{0:T(128)} %get-tuple-element.74.box, s32[2]{0:T(128)} %get-tuple-element.75.bits, s32[2,32,128]{2,1,0:T(8,128)} %get-tuple-element.76.patterns, s32[32,128]{1,0:T(8,128)} %get-tuple-element.77.targets, bf16[2,2048,128]{2,1,0:T(8,128)(2,1)} %get-tuple-element.78.weights_hbm, ...), custom_call_target="tpu_custom_call" | custom-call | flops 4294967296 | bytes 8388608 | tf_op jit(solution)/shard_map/cond/branch_1_fun/pallas_call | solution.py:208
  65.8 0.6 copy.17
Async XLA Ops:
  0.0 4.6 %collective-permute-start = (s32[2]{0:T(128)}, s32[2]{0:T(128)S(1)}, u32[]{:S(2)}, u32[]{:S(2)}) collective-permute-start(s32[2]{0:T(128)} %param.16), channel_id=1, source_target_pairs={{0,16},{16,0},{1,17},{17,1},{2,18},{18,2},{3,19},{19,3},{4,20},{20... | collective-permute-start | bytes 32 | tf_op jit(solution)/shard_map/ppermute | solution.py:252
